TPU v7x, 128 devices: a whole 4x4x4 slice. The times are simulated.
128 devices in a mesh: row: 16 (over y, x), col: 8 (over z, core).
Axes of the slice: x: 4, y: 4, z: 4, core: 2. Of those that a mesh axis runs over, the one named last changes fastest.
Arguments:
- inputs: bfloat16 [1024, 8192], P('col', 'row'), may hold values from -6 to 6
- out_grad: bfloat16 [1024, 8192], P('col', 'row'), may hold values from -1.5 to 1.5
- gate_pre: bfloat16 [1024, 14336], P('row', 'col'), may hold values from -9 to 9
- up_pre: bfloat16 [1024, 14336], P('row', 'col'), may hold values from -6 to 6
- gate_weight: bfloat16 [8192, 14336], P('row', 'col'), may hold values from -0.0625 to 0.0625
- up_weight: bfloat16 [8192, 14336], P('row', 'col'), may hold values from -0.0625 to 0.0625
- down_weight: bfloat16 [14336, 8192], P('col', 'row'), may hold values from -0.046875 to 0.046875
Outputs:
- input_grad: float32 [1024, 8192], P('col', 'row')
- gate_grad: float32 [8192, 14336], P('row', 'col')
- up_grad: float32 [8192, 14336], P('row', 'col')
- down_grad: float32 [14336, 8192], P('col', 'row')
All inputs are finite; a program needn't handle non-finite values.
Results may differ from a plain program's by a relative error of at most 0.0029.
Values may be sent and summed in bfloat16 or wider, within the bound.
A program may use at most 128 MiB of HBM per device.

v0:
```python
import jax
import jax.numpy as jnp
from jax import lax
from jax.sharding import PartitionSpec as P

LEAD_DIMS = (((0,), (0,)), ((), ()))
LAST_DIMS = (((1,), (1,)), ((), ()))


def swiglu_grads(grad_hidden, gate_pre, up_pre):
    gate_val = gate_pre.astype(jnp.float32)
    up_val = up_pre.astype(jnp.float32)
    gate_sig = jax.nn.sigmoid(gate_val)
    hidden = (gate_val * gate_sig * up_val).astype(jnp.bfloat16)
    grad_gate = (grad_hidden * up_val * gate_sig * (1.0 + gate_val * (1.0 - gate_sig))).astype(
        jnp.bfloat16
    )
    grad_up = (grad_hidden * gate_val * gate_sig).astype(jnp.bfloat16)
    return (hidden, grad_gate, grad_up)


def body(inputs, out_grad, gate_pre, up_pre, gate_weight, up_weight, down_weight):
    input_full, grad_full = (
        lax.all_gather(inputs, "col", axis=0, tiled=True),
        lax.all_gather(out_grad, "col", axis=0, tiled=True),
    )
    partial_sum = lax.dot_general(
        grad_full, down_weight, LAST_DIMS, preferred_element_type=jnp.float32
    )
    grad_hidden = lax.psum(partial_sum, "row")
    gate_all, up_all = (
        lax.all_gather(gate_pre, "row", axis=0, tiled=True),
        lax.all_gather(up_pre, "row", axis=0, tiled=True),
    )
    hidden, grad_gate, grad_up = swiglu_grads(grad_hidden, gate_all, up_all)
    total = lax.dot_general(grad_gate, gate_weight, LAST_DIMS, preferred_element_type=jnp.float32)
    input_grad = lax.psum_scatter(
        total + lax.dot_general(grad_up, up_weight, LAST_DIMS, preferred_element_type=jnp.float32),
        "col",
        scatter_dimension=0,
        tiled=True,
    )
    gate_grad = lax.dot_general(
        input_full, grad_gate, LEAD_DIMS, preferred_element_type=jnp.float32
    )
    up_grad = lax.dot_general(input_full, grad_up, LEAD_DIMS, preferred_element_type=jnp.float32)
    down_grad = lax.dot_general(hidden, grad_full, LEAD_DIMS, preferred_element_type=jnp.float32)
    return (input_grad, gate_grad, up_grad, down_grad)


def solution(mesh):
    in_specs = (
        P("col", "row"),
        P("col", "row"),
        P("row", "col"),
        P("row", "col"),
        P("row", "col"),
        P("row", "col"),
        P("col", "row"),
    )
    out_specs = (P("col", "row"), P("row", "col"), P("row", "col"), P("col", "row"))
    return jax.shard_map(body, mesh=mesh, in_specs=in_specs, out_specs=out_specs, check_vma=False)
```

profile of v0, /device:TPU:0, one launch (start us, length us, event | category | flops | bytes accessed | tf_op | source)
XLA Modules:
  0.0 340.9 jit_solution(9743817639233089111)
XLA Ops:
  7.2 0.0 copy-start
  7.2 0.0 all-gather.5.cloned.1.call-start
  7.2 0.7 all-gather.5.cloned.1.call-update
  7.9 0.0 all-gather.7.cloned.1.call-start
  8.0 0.7 all-gather.7.cloned.1.call-update
  8.7 0.0 all-gather.9.cloned.1.call-start
  8.7 0.7 all-gather.9.cloned.1.call-update
  9.4 0.0 all-reduce.2.cloned.1.call-start
  9.4 26.4 %all-gather.5.cloned.1.call-done = bf16[1024,512]{1,0:T(8,128)(2,1)} async-done(((bf16[128,512]{1,0:T(8,128)(2,1)}), bf16[1024,512]{1,0:T(8,128)(2,1)}) %all-gather.5.cloned.1.call-update) | async-done | bytes 1048592 | tf_op jit(solution)/shard_map/all_gather | solution.py:25
  35.8 0.0 copy-done
  35.8 6.4 %fusion.13 = f32[1024,1792]{1,0:T(8,128)} fusion(bf16[1024,512]{1,0:T(8,128)(2,1)} %all-gather.5.cloned.1.call-done, bf16[1792,512]{1,0:T(8,128)(2,1)S(1)} %copy-done), kind=kOutput, calls=%fused_computation.21 | convolution fusion | flops 1879048192 | bytes 10223616 | tf_op jit(solution)/shard_map/dot_general | solution.py:27
  42.2 0.0 all-reduce.2.cloned.1.call-update
  42.2 0.0 all-gather.11.cloned.1.call-start
  42.2 0.5 all-gather.11.cloned.1.call-update
  42.8 0.0 reduce-scatter.2.cloned.1.call-start
  42.8 44.6 %all-gather.7.cloned.1.call-done = bf16[1024,1792]{1,0:T(8,128)(2,1)} async-done(((bf16[64,1792]{1,0:T(8,128)(2,1)}), bf16[1024,1792]{1,0:T(8,128)(2,1)}) %all-gather.7.cloned.1.call-update) | async-done | bytes 3670032 | tf_op jit(solution)/shard_map/all_gather | solution.py:33
  87.4 50.9 %all-gather.9.cloned.1.call-done = bf16[1024,1792]{1,0:T(8,128)(2,1)} async-done(((bf16[64,1792]{1,0:T(8,128)(2,1)}), bf16[1024,1792]{1,0:T(8,128)(2,1)}) %all-gather.9.cloned.1.call-update) | async-done | bytes 3670032 | tf_op jit(solution)/shard_map/all_gather | solution.py:32
  138.3 133.8 %all-reduce.2.cloned.1.call-done = f32[1024,1792]{1,0:T(8,128)} async-done(((f32[1024,1792]{1,0:T(8,128)}), f32[1024,1792]{1,0:T(8,128)}) %all-reduce.2.cloned.1.call-update) | async-done | bytes 7340048 | tf_op jit(solution)/shard_map/psum | solution.py:30
  272.2 7.1 %fusion.9 = (bf16[1024,1792]{1,0:T(8,128)(2,1)S(1)}, bf16[1024,1792]{1,0:T(8,128)(2,1)S(1)}) fusion(f32[1024,1792]{1,0:T(8,128)} %all-reduce.2.cloned.1.call-done, bf16[1024,1792]{1,0:T(8,128)(2,1)} %all-gather.9.cloned.1.call-done, bf16[1024,1792]{1,0:T(8,128)(2,1)} %all-gather.7.cloned.1.call-done), kind=kLoop, calls=%fused_computation.15 | loop fusion | flops 27525120 | bytes 22020096 | tf_op jit(solution)/shard_map/convert_element_type | solution.py:18
  279.3 0.0 copy-start.2
  279.3 0.0 copy-start.4
  279.4 2.1 fusion.14
  281.5 1.1 copy-done.1
  282.5 3.5 %convolution_add_fusion = f32[1024,512]{1,0:T(8,128)} fusion(f32[1024,512]{1,0:T(8,128)S(1)} %fusion.14, bf16[1024,1792]{1,0:T(8,128)(2,1)S(1)} %get-tuple-element.8, bf16[512,1792]{1,0:T(8,128)(2,1)S(1)} %copy-done.4), kind=kOutput, calls=%fused_computation.19 | convolution fusion | flops 1879572480 | bytes 9699328 | tf_op jit(solution)/shard_map/dot_general | solution.py:38
  286.0 0.0 reduce-scatter.2.cloned.1.call-update
  286.0 7.8 %fusion.10 = f32[1792,512]{1,0:T(8,128)} fusion(bf16[1024,512]{1,0:T(8,128)(2,1)S(1)} %copy-done.5, bf16[1024,1792]{1,0:T(8,128)(2,1)} %all-gather.7.cloned.1.call-done, bf16[1024,1792]{1,0:T(8,128)(2,1)} %all-gather.9.cloned.1.call-done), kind=kOutput, calls=%fused_computation.16 | convolution fusion | flops 1893728256 | bytes 12058624 | tf_op jit(solution)/shard_map/dot_general | solution.py:47
  293.9 3.4 all-gather.11.cloned.1.call-done
  297.3 6.3 %convolution_bitcast_fusion.1 = f32[512,1792]{0,1:T(8,128)} fusion(bf16[1024,1792]{1,0:T(8,128)(2,1)} %copy-done.2, bf16[1024,512]{1,0:T(8,128)(2,1)} %all-gather.11.cloned.1.call-done), kind=kOutput, calls=%fused_computation.18 | convolution fusion | flops 1879048192 | bytes 8388608 | tf_op jit(solution)/shard_map/dot_general | solution.py:43
  303.5 5.2 %copy.11 = f32[512,1792]{1,0:T(8,128)} copy(f32[512,1792]{0,1:T(8,128)} %convolution_bitcast_fusion.1) | data formatting | bytes 7340032
  308.7 6.0 %convolution_bitcast_fusion = f32[512,1792]{0,1:T(8,128)} fusion(bf16[1024,1792]{1,0:T(8,128)(2,1)} %copy-done.1, bf16[1024,512]{1,0:T(8,128)(2,1)S(1)} %copy-done.6), kind=kOutput, calls=%fused_computation.17 | convolution fusion | flops 1879048192 | bytes 8388608 | tf_op jit(solution)/shard_map/dot_general | solution.py:46
  314.7 5.2 %copy.12 = f32[512,1792]{1,0:T(8,128)} copy(f32[512,1792]{0,1:T(8,128)} %convolution_bitcast_fusion) | data formatting | bytes 7340032
  319.9 14.1 %reduce-scatter.2.cloned.1.call-done = f32[128,512]{1,0:T(8,128)} async-done(((f32[1024,512]{1,0:T(8,128)}), f32[128,512]{1,0:T(8,128)}) %reduce-scatter.2.cloned.1.call-update) | async-done | bytes 262160 | tf_op jit(solution)/shard_map/reduce_scatter | solution.py:37
  (9 shorter events, 0.0 us)
Async XLA Ops:
  7.2 28.6 %copy-start = (bf16[1792,512]{1,0:T(8,128)(2,1)S(1)}, bf16[1792,512]{1,0:T(8,128)(2,1)}, u32[]{:S(2)}) copy-start(bf16[1792,512]{1,0:T(8,128)(2,1)} %param.13) | copy-start | bytes 5505028
  7.2 28.6 %all-gather.5.cloned.1.call-start = ((), (), s32[]{:S(2)}) async-start(), calls=%async_computation.1 | async-start | bytes 1179648 | tf_op jit(solution)/shard_map/all_gather | solution.py:25
  7.9 79.5 %all-gather.7.cloned.1.call-start = ((), (), s32[]{:S(2)}) async-start(), calls=%async_computation.3 | async-start | bytes 3899392 | tf_op jit(solution)/shard_map/all_gather | solution.py:33
  8.7 129.7 %all-gather.9.cloned.1.call-start = ((), (), s32[]{:S(2)}) async-start(), calls=%async_computation.4 | async-start | bytes 3899392 | tf_op jit(solution)/shard_map/all_gather | solution.py:32
  9.4 262.8 %all-reduce.2.cloned.1.call-start = ((), (), s32[]{:S(2)}) async-start(), calls=%async_computation.2 | async-start | bytes 14680064 | tf_op jit(solution)/shard_map/psum | solution.py:30
  42.2 255.1 %all-gather.11.cloned.1.call-start = ((), (), s32[]{:S(2)}) async-start(), calls=%async_computation.6 | async-start | bytes 1179648 | tf_op jit(solution)/shard_map/all_gather | solution.py:24
  42.8 291.3 %reduce-scatter.2.cloned.1.call-start = ((), (), s32[]{:S(2)}) async-start(), calls=%async_computation.5 | async-start | bytes 2359296 | tf_op jit(solution)/shard_map/reduce_scatter | solution.py:37
  272.2 7.2 %copy-start.3 = (bf16[512,1792]{1,0:T(8,128)(2,1)S(1)}, bf16[512,1792]{1,0:T(8,128)(2,1)}, u32[]{:S(2)}) copy-start(bf16[512,1792]{1,0:T(8,128)(2,1)} %param.11) | copy-start | bytes 5505028
  279.3 2.1 copy-start.2
  279.3 3.2 copy-start.1
  279.3 3.2 copy-start.4
  282.5 3.5 %copy-start.5 = (bf16[1024,512]{1,0:T(8,128)(2,1)S(1)}, bf16[1024,512]{1,0:T(8,128)(2,1)}, u32[]{:S(2)}) copy-start(bf16[1024,512]{1,0:T(8,128)(2,1)} %all-gather.5.cloned.1.call-done) | copy-start | bytes 3145732
  303.5 5.2 %copy-start.6 = (bf16[1024,512]{1,0:T(8,128)(2,1)S(1)}, bf16[1024,512]{1,0:T(8,128)(2,1)}, u32[]{:S(2)}) copy-start(bf16[1024,512]{1,0:T(8,128)(2,1)} %all-gather.11.cloned.1.call-done) | copy-start | bytes 3145732
Sparse Core Ops, SparseCore 0:
  9.7 26.0 all-gather.4
  37.9 49.4 all-gather.6
  89.5 48.7 all-gather.8
  141.6 130.4 all-reduce.1
  273.8 23.3 all-gather.10
  300.2 33.7 reduce-scatter.1
where the time goes:
time: 341 us
  waiting for transfers between devices  276 us (81%)
  matrix products  32 us (9%)
  between operations  14.2 us (4%)
  local copies, waits for them, and re-layouts  11.4 us (3%)
  other arithmetic  7.15 us (2%)
    psum x1, waiting for transfers between devices, body(): grad_hidden = lax.psum(partial_sum, 'row')  134 us
    all_gather x1, waiting for transfers between devices, body(): lax.all_gather(gate_pre, 'row', axis=0, tiled=True)  50.9 us
    all_gather x1, waiting for transfers between devices, body(): lax.all_gather(up_pre, 'row', axis=0, tiled=True)  44.6 us
    all_gather x1, waiting for transfers between devices, body(): lax.all_gather(out_grad, 'col', axis=0, tiled=True)  26.4 us
    reduce_scatter x1, waiting for transfers between devices, body(): lax.psum_scatter(total + lax.dot_general(grad_up, up_weight, LAST_DIMS, p...  14.1 us
    unnamed x16, local copies, waits for them, and re-layouts  11.4 us
    dot_general x1, matrix products, body(): lax.dot_general(hidden, grad_full, LEAD_DIMS, preferred_element_type=jnp....  7.83 us
    convert_element_type x1, other arithmetic, swiglu_grads(): grad_up = (grad_hidden * gate_val * gate_sig).astype(jnp.bfloat16)  7.15 us
  transfers between devices with their start and end apart: 6, of which 6 were waited for; matrix products, arithmetic and copies ran while one was open for 15% of the time, Pallas kernels for 0%

commit v1 on v0

--- a/solution.py
+++ b/solution.py
@@ -5,6 +5,15 @@
 
 LEAD_DIMS = (((0,), (0,)), ((), ()))
 LAST_DIMS = (((1,), (1,)), ((), ()))
+
+
+def doubling_sum(array, axis):
+    size = lax.axis_size(axis)
+    result, reach = (array, 1)
+    while reach < size:
+        result = result + lax.ppermute(result, axis, [(i, i ^ reach) for i in range(size)])
+        reach = 2 * reach
+    return result
 
 
 def swiglu_grads(grad_hidden, gate_pre, up_pre):
@@ -27,7 +36,7 @@
     partial_sum = lax.dot_general(
         grad_full, down_weight, LAST_DIMS, preferred_element_type=jnp.float32
     )
-    grad_hidden = lax.psum(partial_sum, "row")
+    grad_hidden = doubling_sum(partial_sum, "row")
     gate_all, up_all = (
         lax.all_gather(gate_pre, "row", axis=0, tiled=True),
         lax.all_gather(up_pre, "row", axis=0, tiled=True),

time: 341 us -> 807 us (2.37)
  waiting for transfers between devices: 276 us -> 709 us
  other arithmetic: 7.15 us -> 31.2 us
  starting transfers between devices: 0.23 us -> 9.49 us
    ppermute x0 -> x4, waiting for transfers between devices: none -> 491 us  [doubling_sum(): lax.ppermute(result, axis, [(i, i ^ reach) for i in range(size)])]
    all_gather x1, waiting for transfers between devices: 50.9 us -> 186 us  [body(): lax.all_gather(gate_pre, 'row', axis=0, tiled=True)]
    psum x1 -> x0, waiting for transfers between devices: 134 us -> none  [body(): grad_hidden = lax.psum(partial_sum, 'row')]
    all_gather x1, waiting for transfers between devices: 44.6 us -> 0.03 us  [body(): lax.all_gather(up_pre, 'row', axis=0, tiled=True)]
    add x0 -> x3, other arithmetic: none -> 22 us  [doubling_sum(): result + lax.ppermute(result, axis, [(i, i ^ reach) for i in range(size)])]
    reduce_scatter x1, waiting for transfers between devices: 14.1 us -> 2.11 us  [body(): lax.psum_scatter(total + lax.dot_general(grad_up, up_weight, LAST_DIMS, p...]
    ppermute x0 -> x4, starting transfers between devices: none -> 9.1 us  [doubling_sum(): lax.ppermute(result, axis, [(i, i ^ reach) for i in range(size)])]
  transfers between devices with their start and end apart: 6 -> 9, of which waited for: 6 -> 7; matrix products, arithmetic and copies ran while one was open for 15% -> 7% of each run, Pallas kernels for 0% -> 0%
where the time goes in v1:
time: 807 us
  waiting for transfers between devices  709 us (88%)
  other arithmetic  31.2 us (4%)
  matrix products  29.2 us (4%)
  between operations  15.8 us (2%)
  local copies, waits for them, and re-layouts  12.8 us (2%)
  starting transfers between devices  9.49 us (1%)
    ppermute x4, waiting for transfers between devices, doubling_sum(): lax.ppermute(result, axis, [(i, i ^ reach) for i in range(size)])  491 us
    all_gather x1, waiting for transfers between devices, body(): lax.all_gather(gate_pre, 'row', axis=0, tiled=True)  186 us
    all_gather x1, waiting for transfers between devices, body(): lax.all_gather(out_grad, 'col', axis=0, tiled=True)  27.8 us
    add x3, other arithmetic, doubling_sum(): result + lax.ppermute(result, axis, [(i, i ^ reach) for i in range(size)])  22 us
  transfers between devices with their start and end apart: 9, of which 7 were waited for; matrix products, arithmetic and copies ran while one was open for 7% of the time, Pallas kernels for 0%

profile of v1, /device:TPU:0, one launch (start us, length us, event | category | flops | bytes accessed | tf_op | source)
XLA Modules:
  0.0 807.1 jit_solution(17971255257563223520)
XLA Ops:
  8.0 0.0 all-gather.5.cloned.1.call-start
  8.1 0.7 all-gather.5.cloned.1.call-update
  8.7 0.0 all-gather.7.cloned.1.call-start
  8.8 27.8 %all-gather.5.cloned.1.call-done = bf16[1024,512]{1,0:T(8,128)(2,1)} async-done(((bf16[128,512]{1,0:T(8,128)(2,1)}), bf16[1024,512]{1,0:T(8,128)(2,1)}) %all-gather.5.cloned.1.call-update) | async-done | bytes 1048592 | tf_op jit(solution)/shard_map/all_gather | solution.py:34
  36.6 3.3 fusion.14
  40.0 1.5 collective-permute-start
  41.5 1.4 copy-done.2
  42.9 157.4 %collective-permute-done = f32[1024,1792]{1,0:T(8,128)} collective-permute-done((f32[1024,1792]{1,0:T(8,128)S(1)}, f32[1024,1792]{1,0:T(8,128)}, u32[]{:S(2)}, u32[]{:S(2)}) %collective-permute-start) | collective-permute-done | bytes 7340064 | tf_op jit(solution)/shard_map/ppermute | solution.py:14
  200.3 6.1 add.23
  206.4 3.1 collective-permute-start.1
  209.4 158.0 %collective-permute-done.1 = f32[1024,1792]{1,0:T(8,128)} collective-permute-done((f32[1024,1792]{1,0:T(8,128)S(1)}, f32[1024,1792]{1,0:T(8,128)}, u32[]{:S(2)}, u32[]{:S(2)}) %collective-permute-start.1) | collective-permute-done | bytes 7340064 | tf_op jit(solution)/shard_map/ppermute | solution.py:14
  367.4 6.9 add.24
  374.3 1.5 collective-permute-start.2
  375.8 0.0 all-gather.9.cloned.1.call-start
  375.9 175.6 %collective-permute-done.2 = f32[1024,1792]{1,0:T(8,128)} collective-permute-done((f32[1024,1792]{1,0:T(8,128)}, f32[1024,1792]{1,0:T(8,128)}, u32[]{:S(2)}, u32[]{:S(2)}) %collective-permute-start.2) | collective-permute-done | bytes 7340064 | tf_op jit(solution)/shard_map/ppermute | solution.py:14
  551.5 9.0 %add.25 = f32[1024,1792]{1,0:T(8,128)} add(f32[1024,1792]{1,0:T(8,128)} %add.24, f32[1024,1792]{1,0:T(8,128)} %collective-permute-done.2) | non-fusion elementwise | flops 1835008 | bytes 22020096 | tf_op jit(solution)/shard_map/add | solution.py:14
  560.5 3.0 collective-permute-start.3
  563.6 0.0 all-gather.11.cloned.1.call-start
  563.6 0.5 all-gather.11.cloned.1.call-update
  564.1 0.2 reduce-scatter.2.cloned.1.call-start
  564.4 186.0 %all-gather.9.cloned.1.call-done = bf16[1024,1792]{1,0:T(8,128)(2,1)} async-done(((bf16[64,1792]{1,0:T(8,128)(2,1)}), bf16[1024,1792]{1,0:T(8,128)(2,1)}) %all-gather.9.cloned.1.call-update) | async-done | bytes 3670032 | tf_op jit(solution)/shard_map/all_gather | solution.py:41
  750.4 9.2 %fusion.9 = (bf16[1024,1792]{1,0:T(8,128)(2,1)S(1)}, bf16[1024,1792]{1,0:T(8,128)(2,1)S(1)}) fusion(bf16[1024,1792]{1,0:T(8,128)(2,1)} %all-gather.9.cloned.1.call-done, f32[1024,1792]{1,0:T(8,128)} %add.25, f32[1024,1792]{1,0:T(8,128)} %collective-permute-done.3, bf16[1024,1792]{1,0:T(8,128)(2,1)} %all-gather.7.cloned.1.call-done), kind=kLoop, calls=%fused_computation.15 | loop fusion | flops 29360128 | bytes 29360128 | tf_op jit(solution)/shard_map/convert_element_type | solution.py:27
  759.7 2.1 fusion.15
  761.8 1.0 copy-done.4
  762.8 3.5 fusion.13
  766.3 7.8 fusion.10
  774.2 0.4 all-gather.11.cloned.1.call-done
  774.6 6.3 convolution_bitcast_fusion.1
  780.8 5.2 copy.11
  786.1 6.2 convolution_bitcast_fusion
  792.2 5.1 copy.12
  797.4 2.1 reduce-scatter.2.cloned.1.call-done
  (21 shorter events, 0.1 us)
Async XLA Ops:
  8.0 28.6 %copy-start = (bf16[1792,512]{1,0:T(8,128)(2,1)S(1)}, bf16[1792,512]{1,0:T(8,128)(2,1)}, u32[]{:S(2)}) copy-start(bf16[1792,512]{1,0:T(8,128)(2,1)} %param.13) | copy-start | bytes 5505028
  8.0 28.6 %all-gather.5.cloned.1.call-start = ((), (), s32[]{:S(2)}) async-start(), calls=%async_computation.1 | async-start | bytes 1179648 | tf_op jit(solution)/shard_map/all_gather | solution.py:34
  8.7 555.7 %all-gather.7.cloned.1.call-start = ((), (), s32[]{:S(2)}) async-start(), calls=%async_computation.2 | async-start | bytes 3899392 | tf_op jit(solution)/shard_map/all_gather | solution.py:42
  40.0 2.9 copy-start.2
  40.0 160.3 %collective-permute-start = (f32[1024,1792]{1,0:T(8,128)S(1)}, f32[1024,1792]{1,0:T(8,128)}, u32[]{:S(2)}, u32[]{:S(2)}) collective-permute-start(f32[1024,1792]{1,0:T(8,128)S(1)} %fusion.14), channel_id=1, source_target_pairs={{0,8},{8,0},{16,24},{24,16},{32,40},{40,32},{48,56},{56,48},{64,72... | collective-permute-start | bytes 22020104 | tf_op jit(solution)/shard_map/ppermute | solution.py:14
  206.4 161.0 %collective-permute-start.1 = (f32[1024,1792]{1,0:T(8,128)S(1)}, f32[1024,1792]{1,0:T(8,128)}, u32[]{:S(2)}, u32[]{:S(2)}) collective-permute-start(f32[1024,1792]{1,0:T(8,128)S(1)} %add.23), channel_id=1, source_target_pairs={{0,16},{8,24},{16,0},{24,8},{32,48},{40,56},{48,32},{56,40},{64,80... | collective-permute-start | bytes 22020104 | tf_op jit(solution)/shard_map/ppermute | solution.py:14
  374.3 177.2 %collective-permute-start.2 = (f32[1024,1792]{1,0:T(8,128)}, f32[1024,1792]{1,0:T(8,128)}, u32[]{:S(2)}, u32[]{:S(2)}) collective-permute-start(f32[1024,1792]{1,0:T(8,128)} %add.24), channel_id=1, source_target_pairs={{0,32},{8,40},{16,48},{24,56},{32,0},{40,8},{48,16},{56,24},{64,96... | collective-permute-start | bytes 22020104 | tf_op jit(solution)/shard_map/ppermute | solution.py:14
  375.8 374.5 %all-gather.9.cloned.1.call-start = ((), (), s32[]{:S(2)}) async-start(), calls=%async_computation.3 | async-start | bytes 3899392 | tf_op jit(solution)/shard_map/all_gather | solution.py:41
  560.5 189.9 %collective-permute-start.3 = (f32[1024,1792]{1,0:T(8,128)}, f32[1024,1792]{1,0:T(8,128)}, u32[]{:S(2)}, u32[]{:S(2)}) collective-permute-start(f32[1024,1792]{1,0:T(8,128)} %add.25), channel_id=1, source_target_pairs={{0,64},{8,72},{16,80},{24,88},{32,96},{40,104},{48,112},{56,120},{... | collective-permute-start | bytes 22020104 | tf_op jit(solution)/shard_map/ppermute | solution.py:14
  563.6 211.0 %all-gather.11.cloned.1.call-start = ((), (), s32[]{:S(2)}) async-start(), calls=%async_computation.5 | async-start | bytes 1179648 | tf_op jit(solution)/shard_map/all_gather | solution.py:33
  564.1 195.5 %copy-start.5 = (bf16[512,1792]{1,0:T(8,128)(2,1)S(1)}, bf16[512,1792]{1,0:T(8,128)(2,1)}, u32[]{:S(2)}) copy-start(bf16[512,1792]{1,0:T(8,128)(2,1)} %param.12) | copy-start | bytes 5505028
  564.1 235.4 %reduce-scatter.2.cloned.1.call-start = ((), (), s32[]{:S(2)}) async-start(), calls=%async_computation.4 | async-start | bytes 2359296 | tf_op jit(solution)/shard_map/reduce_scatter | solution.py:46
  759.7 2.1 copy-start.3
  759.7 3.1 copy-start.4
  759.7 3.1 copy-start.6
  762.8 3.6 copy-start.7
  780.8 5.2 copy-start.8
  786.1 13.4 %copy-start.1 = (bf16[1792,512]{1,0:T(8,128)(2,1)S(1)}, bf16[1792,512]{1,0:T(8,128)(2,1)}, u32[]{:S(2)}) copy-start(bf16[1792,512]{1,0:T(8,128)(2,1)} %param.13) | copy-start | bytes 5505028
Sparse Core Ops, SparseCore 0:
  10.6 26.0 all-gather.4
  766.5 32.9 reduce-scatter.1
Sparse Core Ops, SparseCore 1:
  375.9 63.0 all-gather.6
  563.6 186.7 all-gather.8
  752.0 22.5 all-gather.10
